TPU v7x, 128 devices: a whole 4x4x4 slice. The times are simulated.
128 devices in a mesh: section: 2 (over y_hi), dp: 32 (over z, x, core), tensor: 2 (over y_lo).
Axes of the slice: x: 4, y: 4 (y_hi: 2, y_lo: 2; y = y_hi * 2 + y_lo), z: 4, core: 2. Of those that a mesh axis runs over, the one named last changes fastest.
Arguments:
- layer_input: bfloat16 [2, 32, 256, 1024], P(None, 'dp'), may hold values from -6 to 6
- cotangent: bfloat16 [2, 32, 256, 1024], P(None, 'dp'), may hold values from -6 to 6
- order: int32 [2], replicated, may hold values from 0 to 1, each once
- ln1_scale: bfloat16 [2, 1024], P('section'), may hold values from 0.099609375 to 1.8984375
- ln1_bias: bfloat16 [2, 1024], P('section'), may hold values from -1.796875 to 1.796875
- ln2_scale: bfloat16 [2, 1024], P('section'), may hold values from 0.099609375 to 1.8984375
- ln2_bias: bfloat16 [2, 1024], P('section'), may hold values from -1.796875 to 1.796875
- qkv_weight: bfloat16 [2, 1024, 3, 1024], P('section', None, None, 'tensor'), may hold values from -0.1875 to 0.1875
- qkv_bias: bfloat16 [2, 3, 1024], P('section', None, 'tensor'), may hold values from -1.796875 to 1.796875
- out_weight: bfloat16 [2, 1024, 1024], P('section', 'tensor'), may hold values from -0.75 to 0.75
- out_bias: bfloat16 [2, 1024], P('section'), may hold values from -3 to 3
- up_weight: bfloat16 [2, 1024, 4096], P('section', None, 'tensor'), may hold values from -0.1875 to 0.1875
- up_bias: bfloat16 [2, 4096], P('section', 'tensor'), may hold values from -3 to 3
- down_weight: bfloat16 [2, 4096, 1024], P('section', 'tensor'), may hold values from -0.09375 to 0.09375
- down_bias: bfloat16 [2, 1024], P('section'), may hold values from -3 to 3
Outputs:
- layer_outputs: bfloat16 [2, 2, 32, 256, 1024], P('section', None, 'dp')
- input_grads: bfloat16 [2, 2, 32, 256, 1024], P('section', None, 'dp')
- ln1_scale_grad: float32 [2, 1024], P('section')
- ln1_bias_grad: float32 [2, 1024], P('section')
- ln2_scale_grad: float32 [2, 1024], P('section')
- ln2_bias_grad: float32 [2, 1024], P('section')
- qkv_weight_grad: float32 [2, 1024, 3, 1024], P('section', None, None, 'tensor')
- qkv_bias_grad: float32 [2, 3, 1024], P('section', None, 'tensor')
- out_weight_grad: float32 [2, 1024, 1024], P('section', 'tensor')
- out_bias_grad: float32 [2, 1024], P('section')
- up_weight_grad: float32 [2, 1024, 4096], P('section', None, 'tensor')
- up_bias_grad: float32 [2, 4096], P('section', 'tensor')
- down_weight_grad: float32 [2, 4096, 1024], P('section', 'tensor')
- down_bias_grad: float32 [2, 1024], P('section')
Inputs may be any that keep to these rules, and one draw needn't show every extreme that they name: order names each of the 2 micro-batches once.
All inputs are finite; a program needn't handle non-finite values.
Results may differ from a plain program's by a relative error of at most 0.023.
Values may be sent and summed in bfloat16 or wider, within the bound.
A program may use at most 192 MiB of HBM per device.

v0:
```python
import jax
import jax.numpy as jnp
import numpy as np
from jax import lax
from jax.experimental import pallas as pl
from jax.experimental.pallas import tpu as pltpu
from jax.sharding import PartitionSpec as P

MESH = pl.DeviceIdType.MESH
VMEM_LIMIT = 50 * 2**20

SLABS = 6
SLAB_ROWS = 2048
HALF = 1024
STREAM = 512
COLS = 512
CHUNK = (128, 32)
RX_ONE = (0, 768)
RX_TWO = (256, 832)
RX_ROWS = 960
SMALL = 32


def mod4(value):
    return lax.rem(value + 4, 4)


class Place:
    def __init__(self):
        self.section = lax.axis_index("section")
        self.tensor = lax.axis_index("tensor")
        dp = lax.axis_index("dp")
        self.core = lax.rem(dp, 2)
        self.x = lax.rem(dp // 2, 4)
        self.z = dp // 8

    def at(self, z, x, core):
        return (self.section, (z * 4 + x) * 2 + core, self.tensor)

    def other_core(self):
        return self.at(self.z, self.x, 1 - self.core)

    def along(self, axis, step):
        if axis == 0:
            return self.at(self.z, mod4(self.x + step), self.core)
        return self.at(mod4(self.z + step), self.x, self.core)

    def position(self, axis):
        return self.x if axis == 0 else self.z


def ds(start, size):
    return pl.ds(pl.multiple_of(start, 16), size)


def take(ref, sem):
    pltpu.make_async_copy(ref, ref, sem).wait()


def put(src, dst, send_sem, recv_sem, device):
    pltpu.make_async_remote_copy(
        src_ref=src, dst_ref=dst, send_sem=send_sem, recv_sem=recv_sem,
        device_id=device, device_id_type=MESH,
    ).start()


def added(*parts):
    total = parts[0].astype(jnp.float32)
    for part in parts[1:]:
        total = total + part.astype(jnp.float32)
    return total.astype(jnp.bfloat16)


class Reduce:
    def __init__(self, place, grads, out, arrived, landing, send, recv):
        self.place, self.grads, self.out = place, grads, out
        self.arrived, self.landing, self.send, self.recv = arrived, landing, send, recv

    def base(self, stream):
        return self.place.core * HALF + stream * STREAM

    def layout(self, stream, phase):
        axis = (stream + phase) % 2
        p = self.place.position(axis)
        start = self.base(stream)
        if phase == 1:
            start = start + self.place.position(stream) * CHUNK[0]
        return axis, p, start, CHUNK[phase]

    def first_sends(self, s, phase, sem):
        h = CHUNK[phase] // 2
        for stream in range(2):
            axis, p, start, size = self.layout(stream, phase)
            far = start + mod4(p + 2) * size
            for side, step in ((0, 1), (1, -1)):
                put(self.grads.at[s, ds(far + side * h, h)],
                    self.landing.at[s, pl.ds(RX_ONE[phase] + (stream * 2 + side) * h, h)],
                    self.send.at[s, 0], self.recv.at[s, sem], self.place.along(axis, step))

    def second_sends(self, s, phase, sem):
        h = CHUNK[phase] // 2
        take(self.landing.at[s, pl.ds(0, 4 * h)], self.recv.at[s, sem - 1])
        for stream in range(2):
            axis, p, start, size = self.layout(stream, phase)
            for side, step in ((0, 1), (1, -1)):
                near = start + mod4(p + step) * size
                rows = ds(near + side * h, h)
                came = pl.ds(RX_ONE[phase] + (stream * 2 + side) * h, h)
                self.grads[s, rows] = added(self.grads[s, rows], self.landing[s, came])
                put(self.grads.at[s, ds(near, size)],
                    self.landing.at[s, pl.ds(RX_TWO[phase] + (stream * 2 + side) * size, size)],
                    self.send.at[s, 0], self.recv.at[s, sem], self.place.along(axis, step))

    def finish(self, s, phase, sem, target):
        size = CHUNK[phase]
        take(self.landing.at[s, pl.ds(0, 4 * size)], self.recv.at[s, sem])
        for stream in range(2):
            axis, p, start, size = self.layout(stream, phase)
            rows = ds(start + p * size, size)
            left = pl.ds(RX_TWO[phase] + stream * 2 * size, size)
            right = pl.ds(RX_TWO[phase] + (stream * 2 + 1) * size, size)
            target[s, rows] = added(self.grads[s, rows], self.landing[s, left], self.landing[s, right])

    def spread(self, s, phase, sem):
        for stream in range(2):
            axis, p, start, size = self.layout(stream, phase)
            rows = ds(start + p * size, size)
            for step in (1, -1):
                put(self.out.at[s, rows], self.out.at[s, rows], self.send.at[s, 1],
                    self.recv.at[s, sem], self.place.along(axis, step))

    def forward(self, s, phase, sem):
        size = CHUNK[phase]
        take(self.out.at[s, pl.ds(0, 4 * size)], self.recv.at[s, sem - 1])
        for stream in range(2):
            axis, p, start, size = self.layout(stream, phase)
            for side, step in ((0, 1), (1, -1)):
                rows = ds(start + mod4(p - step) * size + side * (size // 2), size // 2)
                put(self.out.at[s, rows], self.out.at[s, rows], self.send.at[s, 1],
                    self.recv.at[s, sem], self.place.along(axis, step))

    def to_core(self, s, offsets):
        for stream in range(2):
            axis, p, start, size = self.layout(stream, 0)
            for offset in offsets:
                rows = ds(start + mod4(p + offset) * size, size)
                put(self.out.at[s, rows], self.out.at[s, rows], self.send.at[s, 1],
                    self.recv.at[s, 9], self.place.other_core())

    def step(self, s, k):
        core = self.place.core
        if k == 0:
            put(self.grads.at[s, ds((1 - core) * HALF, HALF)], self.arrived.at[s],
                self.send.at[s, 0], self.recv.at[s, 0], self.place.other_core())
        elif k == 1:
            take(self.arrived.at[s], self.recv.at[s, 0])

            def block(i, _):
                here = ds(core * HALF + i * 128, 128)
                self.grads[s, here] = added(self.grads[s, here], self.arrived[s, ds(i * 128, 128)])
                return 0

            lax.fori_loop(0, HALF // 128, block, 0)
            self.first_sends(s, 0, 1)
        elif k == 2:
            self.second_sends(s, 0, 2)
        elif k == 3:
            self.finish(s, 0, 2, self.grads)
            self.first_sends(s, 1, 3)
        elif k == 4:
            self.second_sends(s, 1, 4)
        elif k == 5:
            self.finish(s, 1, 4, self.out)
            self.spread(s, 1, 5)
        elif k == 6:
            self.forward(s, 1, 6)
        elif k == 7:
            take(self.out.at[s, pl.ds(0, 64)], self.recv.at[s, 6])
            self.spread(s, 0, 7)
            self.to_core(s, (0,))
        elif k == 8:
            self.forward(s, 0, 8)
            self.to_core(s, (1, -1))
        elif k == 9:
            take(self.out.at[s, pl.ds(0, 256)], self.recv.at[s, 8])
            self.to_core(s, (2,))
        elif k == 10:
            take(self.out.at[s, pl.ds(0, 1024)], self.recv.at[s, 9])

    def drain(self, s):
        take(self.grads.at[s, pl.ds(0, 1984)], self.send.at[s, 0])
        take(self.grads.at[s, pl.ds(0, 1984)], self.send.at[s, 1])


class SmallReduce:
    def __init__(self, place, mine, out, landing, pair, send, recv):
        self.place, self.mine, self.out, self.landing, self.pair = place, mine, out, landing, pair
        self.send, self.recv = send, recv

    def exchange(self, axis):
        p = self.place.position(axis)
        for step in (1, 2, 3):
            put(self.landing.at[axis, p], self.landing.at[axis, p], self.send, self.recv.at[1 + axis],
                self.place.along(axis, step))

    def collected(self, axis):
        take(self.landing.at[axis, pl.ds(0, 3)], self.recv.at[1 + axis])
        return added(*[self.landing[axis, j] for j in range(4)])

    def step(self, k):
        half = SMALL // 2
        rows = ds(self.place.core * half, half)
        if k == 0:
            put(self.mine, self.pair, self.send, self.recv.at[0], self.place.other_core())
        elif k == 1:
            take(self.pair, self.recv.at[0])
            self.landing[0, self.place.x] = added(self.mine[rows], self.pair[rows])
            self.exchange(0)
        elif k == 2:
            self.landing[1, self.place.z] = self.collected(0)
            self.exchange(1)
        elif k == 3:
            self.out[rows] = self.collected(1)
            put(self.out.at[rows], self.out.at[rows], self.send, self.recv.at[3], self.place.other_core())
        elif k == 4:
            take(self.out.at[pl.ds(0, half)], self.recv.at[3])

    def drain(self):
        half = SMALL // 2
        take(self.landing.at[0, pl.ds(0, 3)], self.send)
        take(self.landing.at[0, pl.ds(0, 3)], self.send)
        take(self.mine, self.send)
        take(self.out.at[pl.ds(0, half)], self.send)


def greet(devices):
    for device in devices:
        pl.semaphore_signal(pltpu.get_barrier_semaphore(), inc=1, device_id=device, device_id_type=MESH)


def met(count):
    pl.semaphore_wait(pltpu.get_barrier_semaphore(), count)


def plane_partners(place):
    return [place.other_core()] + [place.along(axis, step) for axis in (0, 1) for step in (1, 2, 3)]


PLAN = (
    "down0", (0, 0), "down1", (1, 0), "back", (0, 1), "up0", (1, 1),
    (2, 0), "up1", (3, 0), (0, 2), "attend", (2, 1), (1, 2), (3, 1),
    (0, 3), "inputs", (2, 2), "last0", (1, 3), (4, 0), "last1", (3, 2),
    (0, 4), (5, 0), "finish0", "finish1", "sums", "copies", (4, 1), (2, 3),
    (1, 4), "norms", "small0", (5, 1), (3, 3), (0, 5), (4, 2), (2, 4),
    (1, 5), (5, 2), (3, 4), (0, 6), "small1", (4, 3), (2, 5), (1, 6),
    (5, 3), (3, 5), (0, 7), (4, 4), (2, 6), "small2", (1, 7), (5, 4),
    (3, 6), (0, 8), (4, 5), (2, 7), (1, 8), (5, 5), "small3", (3, 7),
    (0, 9), (4, 6), (2, 8), (1, 9), (5, 6), (3, 8), (4, 7), "small4",
    (2, 9), (5, 7), (3, 9), (4, 8), (5, 8), (4, 9), (5, 9),
)

SEQ = 256
TOKENS = 2 * SEQ
OWN = SEQ // 2
PARTS = 8
PART = OWN // PARTS
WIDTH = 1024
HEAD = 64
ROT = 16
EPSILON = 1e-05
BF16 = jnp.bfloat16
F32 = jnp.float32


def nn(a, b):
    return lax.dot_general(a, b, (((1,), (0,)), ((), ())), preferred_element_type=F32)


def nt(a, b):
    return lax.dot_general(a, b, (((1,), (1,)), ((), ())), preferred_element_type=F32)


def tn(a, b):
    return lax.dot_general(a, b, (((0,), (0,)), ((), ())), preferred_element_type=F32)


def wide(ref):
    return ref[...].astype(F32)


def block(index, size):
    return pl.ds(pl.multiple_of(index * size, size), size)


def one_head(pair, h):
    lane = lax.broadcasted_iota(jnp.int32, pair.shape, 1)
    return jnp.where((lane < HEAD) if h == 0 else (lane >= HEAD), pair, jnp.zeros_like(pair))


def rotary_tables():
    frequency = (1.0 / 10000.0 ** (np.arange(ROT // 2) * 2.0 / ROT)).astype(np.float32)
    angles = np.arange(SEQ, dtype=np.float32)[:, None] * frequency[None, :]
    cos, sin = np.cos(angles), np.sin(angles)
    cos_table = np.ones((SEQ, 128), np.float32)
    low_sin, high_sin = np.zeros((SEQ, 128), np.float32), np.zeros((SEQ, 128), np.float32)
    for head in range(128 // HEAD):
        first, second = head * HEAD, head * HEAD + ROT // 2
        cos_table[:, first:second] = cos
        cos_table[:, second:second + ROT // 2] = cos
        low_sin[:, first:second] = sin
        high_sin[:, second:second + ROT // 2] = sin
    return cos_table, low_sin, high_sin


def rotated(u, tables, sign):
    cos, low_sin, high_sin = tables
    ahead = pltpu.roll(u, 128 - ROT // 2, 1)
    behind = pltpu.roll(u, ROT // 2, 1)
    return u * cos + (behind * high_sin - ahead * low_sin) * sign


class Layer:
    def __init__(self, refs):
        self.__dict__.update(refs)

    def up_block(self, n, rows):
        return self.out.at[4 + n // 2, pl.ds((n % 2) * WIDTH + rows[0], rows[1])]

    def slope_block(self, m, n):
        return self.grads.at[4, ds(n * COLS + m * SEQ, SEQ)]

    def norm(self, m):
        rows = block(m, SEQ)
        x = wide(self.x.at[rows])
        mean = jnp.mean(x, axis=1, keepdims=True)
        centered = x - mean
        rstd = lax.rsqrt(jnp.mean(centered * centered, axis=1, keepdims=True) + EPSILON)
        normed = centered * rstd
        self.mean[rows] = mean
        self.rstd[rows] = rstd
        self.first_in[rows] = (normed * wide(self.ln1_scale) + wide(self.ln1_bias)).astype(BF16)
        self.second_in[rows] = (normed * wide(self.ln2_scale) + wide(self.ln2_bias)).astype(BF16)

    def project(self, m):
        rows = block(m, SEQ)
        tables = (self.cos[...], self.low_sin[...], self.high_sin[...])
        bias = wide(self.qkv_bias)
        for t in range(3):
            part = nn(self.first_in[rows], self.qkv_w[t]) + bias[t:t + 1]
            for lane in range(0, COLS, 128):
                piece = part[:, lane:lane + 128]
                if t < 2:
                    piece = rotated(piece, tables, 1.0)
                if t == 0:
                    piece = piece * HEAD ** -0.5
                self.qkv[t, rows, pl.ds(lane, 128)] = piece.astype(BF16)

    def attend(self, m):
        rows = block(m, SEQ)
        causal = (lax.broadcasted_iota(jnp.int32, (SEQ, SEQ), 0)
                  >= lax.broadcasted_iota(jnp.int32, (SEQ, SEQ), 1))
        for hp in range(4):
            lanes = pl.ds(hp * 128, 128)
            q, k, v = (self.qkv[t, rows, lanes] for t in range(3))
            context = None
            for h in range(2):
                scores = jnp.where(causal, nt(one_head(q, h), k), -1e30)
                exp = jnp.exp(scores - jnp.max(scores, axis=1, keepdims=True))
                probs = (exp * (1.0 / jnp.sum(exp, axis=1, keepdims=True))).astype(BF16)
                self.probs[m, hp * 2 + h] = probs
                part = nn(probs, one_head(v, h))
                context = part if context is None else context + part
            self.context[rows, lanes] = context.astype(BF16)

    def up(self, m):
        rows = block(m, SEQ)
        bias = wide(self.up_bias)
        for n in range(4):
            hidden = nn(self.second_in[rows], self.up_block(n, (0, WIDTH))[...])
            hidden = hidden + bias[:, n * COLS:(n + 1) * COLS]
            cdf = 0.5 * (1.0 + lax.erf(hidden * 0.7071067811865476))
            density = jnp.exp(-0.5 * hidden * hidden) * 0.3989422804014327
            lanes = pl.ds(n * COLS, COLS)
            self.activated[rows, lanes] = (hidden * cdf).astype(BF16)
            self.slope_block(m, n)[...] = (cdf + hidden * density).astype(BF16)

    def branches(self, m):
        rows = block(m, SEQ)
        for j in range(2):
            lanes = pl.ds(j * COLS, COLS)
            total = nn(self.context[rows], self.out_w[:, lanes])
            total = total + nn(self.activated[rows], self.out[2 + j])
            self.partial[m, :, lanes] = total.astype(BF16)

    def back_branches(self, m):
        rows = block(m, SEQ)
        upstream = self.upstream[rows]
        self.d_context[rows] = nt(upstream, self.out_w[...]).astype(BF16)
        for n in range(4):
            down = pl.ds(n * COLS, COLS)
            part = nt(upstream[:, :COLS], self.out[2, down]) + nt(upstream[:, COLS:], self.out[3, down])
            self.d_hidden[rows, down] = part.astype(BF16)

    def back_gelu(self, m):
        rows = block(m, SEQ)
        for n in range(4):
            lanes = pl.ds(n * COLS, COLS)
            self.d_hidden[rows, lanes] = (
                wide(self.d_hidden.at[rows, lanes]) * wide(self.slope_block(m, n))
            ).astype(BF16)

    def back_attend(self, m):
        rows = block(m, SEQ)
        tables = (self.cos[...], self.low_sin[...], self.high_sin[...])
        for hp in range(4):
            lanes = pl.ds(hp * 128, 128)
            q, k, v = (self.qkv[t, rows, lanes] for t in range(3))
            d_context = self.d_context[rows, lanes]
            probs = [self.probs[m, hp * 2 + h] for h in range(2)]
            d_mine = [one_head(d_context, h) for h in range(2)]
            d_scores = []
            for h in range(2):
                wide_probs = probs[h].astype(F32)
                weighted = nt(d_mine[h], v) * wide_probs
                inner = jnp.sum(weighted, axis=1, keepdims=True)
                d_scores.append((weighted - wide_probs * inner).astype(BF16))
            both = [jnp.concatenate([one_head(u, 0), one_head(u, 1)], axis=0) for u in (q, k)]
            d_query = nn(jnp.concatenate(d_scores, axis=1), both[1])
            d_key = tn(jnp.concatenate(d_scores, axis=0), both[0])
            d_value = tn(jnp.concatenate(probs, axis=0), jnp.concatenate(d_mine, axis=0))
            d_query = rotated(d_query * HEAD ** -0.5, tables, -1.0)
            d_key = rotated(d_key, tables, -1.0)
            for t, part in enumerate((d_query, d_key, d_value)):
                self.d_projected[t, rows, lanes] = part.astype(BF16)

    def back_inputs(self, m):
        rows = block(m, SEQ)
        mean, rstd = self.mean[rows], self.rstd[rows]
        for j in range(2):
            lanes = pl.ds(j * COLS, COLS)
            d_second = None
            for n in range(4):
                part = nt(self.d_hidden[rows, pl.ds(n * COLS, COLS)], self.up_block(n, (j * COLS, COLS))[...])
                d_second = part if d_second is None else d_second + part
            d_first = None
            for t in range(3):
                part = nt(self.d_projected[t, rows], self.qkv_w[t, lanes])
                d_first = part if d_first is None else d_first + part
            normed = (wide(self.x.at[rows, lanes]) - mean) * rstd
            sums = (d_first * normed, d_first, d_second * normed, d_second)
            for i, value in enumerate(sums):
                row = pl.ds(2 * i + j, 1)
                self.vectors[row] = self.vectors[row] + jnp.sum(value, axis=0, keepdims=True)
            d_normed = d_first * wide(self.ln1_scale.at[:, lanes]) + d_second * wide(self.ln2_scale.at[:, lanes])
            self.partial[m, :, lanes] = d_normed.astype(BF16)

    def weight_sum(self, name):
        def product(left, columns, targets):
            turned = left[:, columns].T
            for right, b in targets:
                self.grads[b // 4, pl.ds((b % 4) * COLS, COLS)] = nn(turned, right).astype(BF16)

        upstream = [self.upstream[:, pl.ds(c * COLS, COLS)] for c in range(2)]
        if name in ("down0", "down1"):
            for r in (0, 1) if name == "down0" else (2, 3):
                product(self.activated, pl.ds(r * COLS, COLS), [(upstream[c], 2 * r + c) for c in range(2)])
        elif name in ("up0", "up1"):
            r = int(name == "up1")
            d_hidden = [self.d_hidden[:, pl.ds(n * COLS, COLS)] for n in range(4)]
            product(self.second_in, pl.ds(r * COLS, COLS), [(d_hidden[n], 8 + 4 * r + n) for n in range(4)])
        else:
            r = int(name == "last1")
            if r == 0:
                product(self.context, pl.ds(0, COLS), [(upstream[c], 16 + c) for c in range(2)])
            d_projected = [self.d_projected[t] for t in range(3)]
            product(self.first_in, pl.ds(r * COLS, COLS), [(d_projected[t], 18 + 3 * r + t) for t in range(3)])

    def bias_sums(self):
        for t in range(3):
            self.vectors[pl.ds(8 + t, 1)] = jnp.sum(wide(self.d_projected.at[t]), axis=0, keepdims=True)
        for j in range(2):
            lanes = pl.ds(j * COLS, COLS)
            self.vectors[pl.ds(11 + j, 1)] = jnp.sum(wide(self.upstream.at[:, lanes]), axis=0, keepdims=True)
        for n in range(4):
            lanes = pl.ds(n * COLS, COLS)
            self.vectors[pl.ds(13 + n, 1)] = jnp.sum(wide(self.d_hidden.at[:, lanes]), axis=0, keepdims=True)


INPUTS = ("x_in", "cot_in", "order", "ln1_scale", "ln1_bias", "ln2_scale", "ln2_bias", "qkv_in", "qkv_bias",
          "out_in", "out_bias", "up_in", "up_bias", "down_in", "down_bias", "cos", "low_sin", "high_sin")
IN_HBM = ("x_in", "cot_in", "qkv_in", "out_in", "up_in", "down_in")
OUTPUTS = ("y_out", "g_out", "out", "small_out")
DMA = pltpu.SemaphoreType.DMA
SCRATCH = dict(
    grads=pltpu.VMEM((SLABS, SLAB_ROWS, COLS), BF16),
    arrived=pltpu.VMEM((SLABS, HALF, COLS), BF16),
    landing=pltpu.VMEM((SLABS, RX_ROWS, COLS), BF16),
    x=pltpu.VMEM((TOKENS, WIDTH), BF16),
    upstream=pltpu.VMEM((TOKENS, WIDTH), BF16),
    first_in=pltpu.VMEM((TOKENS, WIDTH), BF16),
    second_in=pltpu.VMEM((TOKENS, WIDTH), BF16),
    qkv=pltpu.VMEM((3, TOKENS, COLS), BF16),
    d_projected=pltpu.VMEM((3, TOKENS, COLS), BF16),
    context=pltpu.VMEM((TOKENS, COLS), BF16),
    d_context=pltpu.VMEM((TOKENS, COLS), BF16),
    probs=pltpu.VMEM((2, 8, SEQ, SEQ), BF16),
    activated=pltpu.VMEM((TOKENS, 4 * COLS), BF16),
    d_hidden=pltpu.VMEM((TOKENS, 4 * COLS), BF16),
    partial=pltpu.VMEM((2, SEQ, WIDTH), BF16),
    came=pltpu.VMEM((2, 2, OWN, WIDTH), BF16),
    mine=pltpu.VMEM((2, 2, OWN, WIDTH), BF16),
    mean=pltpu.VMEM((TOKENS, 1), F32),
    rstd=pltpu.VMEM((TOKENS, 1), F32),
    vectors=pltpu.VMEM((SMALL, COLS), F32),
    qkv_w=pltpu.VMEM((3, WIDTH, COLS), BF16),
    out_w=pltpu.VMEM((COLS, WIDTH), BF16),
    small_mine=pltpu.VMEM((SMALL, COLS), BF16),
    small_landing=pltpu.VMEM((2, 4, SMALL // 2, COLS), BF16),
    small_pair=pltpu.VMEM((SMALL, COLS), BF16),
    norms=pltpu.VMEM((2, 16, COLS), BF16),
    send=DMA((SLABS, 2)),
    recv=DMA((SLABS, 10)),
    small_send=DMA,
    small_recv=DMA((4,)),
    load=DMA((5,)),
    pair_send=DMA((2, 2)),
    pair_recv=DMA((2, 2, PARTS)),
    next_send=DMA((2,)),
    next_recv=DMA((2, PARTS)),
    far_send=DMA((2,)),
    far_recv=DMA((2,)),
    copy_send=DMA((2, 2)),
    copy_recv=DMA((2, 2)),
    copy_own=DMA((2, 2)),
    norms_sem=DMA((2,)),
)


class Refs:
    def __init__(self, pairs):
        self.__dict__.update(pairs)


def layer_kernel(*refs):
    names = INPUTS + OUTPUTS + tuple(SCRATCH)
    r = Refs(zip(names, refs))
    layer = Layer(vars(r))
    place = Place()
    section, tensor = place.section, place.tensor
    first, last = section == 0, section == 1
    dp = lax.axis_index("dp")
    partner = (section, dp, 1 - tensor)
    near = (1 - section, dp, 1 - tensor)
    others = plane_partners(place) + [partner, near]
    load = r.load
    out, x, upstream = r.out, r.x, r.upstream

    greet(others)

    def fetch(src, dst, sem):
        pltpu.make_async_copy(src, dst, load.at[sem]).start()

    def fetch_out():
        fetch(r.out_in, r.out_w, 3)
        for c in range(2):
            fetch(r.down_in.at[:, pl.ds(c * COLS, COLS)], out.at[2 + c], 4)

    def fetch_up():
        for n in range(4):
            fetch(r.up_in.at[:, pl.ds(n * COLS, COLS)], layer.up_block(n, (0, WIDTH)), 2)

    @pl.when(first)
    def _():
        fetch(r.x_in, x, 0)
        fetch(r.qkv_in, r.qkv_w, 1)
        take(x, load.at[0])
        fetch_up()
        fetch_out()

    @pl.when(last)
    def _():
        fetch(r.cot_in, r.activated.at[:, pl.ds(0, WIDTH)], 0)
        fetch_out()
        fetch(r.qkv_in, r.qkv_w, 1)
        fetch_up()

    @pl.when(last)
    def _():
        given = r.activated
        take(upstream, load.at[0])
        swap = r.order[0] != 0
        one, two = given[pl.ds(0, SEQ), pl.ds(0, WIDTH)], given[pl.ds(SEQ, SEQ), pl.ds(0, WIDTH)]
        upstream[pl.ds(0, SEQ)] = jnp.where(swap, two, one)
        upstream[pl.ds(SEQ, SEQ)] = jnp.where(swap, one, two)
        take(r.out_w, load.at[3])
        take(out.at[pl.ds(2, 2)], load.at[4])

        def each(m, _):
            layer.back_branches(m)
            return 0

        lax.fori_loop(0, 2, each, 0)
        met(len(others))

    r.vectors[...] = jnp.zeros((SMALL, COLS), F32)

    def part_of(start, c):
        return ds(start + c * PART, PART)

    def exchange(m, kind):
        for c in range(PARTS):
            put(r.partial.at[m, part_of((1 - tensor) * OWN, c)], r.came.at[kind, m, part_of(0, c)],
                r.pair_send.at[kind, m], r.pair_recv.at[kind, m, c], partner)

    def finish_part(m, kind, c):
        rows = part_of(m * SEQ + tensor * OWN, c)
        here = part_of(0, c)
        came = r.came.at[kind, m, here]
        take(came, r.pair_recv.at[kind, m, c])
        total = wide(r.partial.at[m, part_of(tensor * OWN, c)]) + wide(came)
        if kind == 0:
            result = wide(x.at[rows]) + total + (wide(r.out_bias) + wide(r.down_bias))
        else:
            rstd = r.rstd[rows]
            normed = (wide(x.at[rows]) - r.mean[rows]) * rstd
            centered = (total - jnp.mean(total, axis=1, keepdims=True)
                        - normed * jnp.mean(total * normed, axis=1, keepdims=True))
            result = wide(upstream.at[rows]) + rstd * centered
        mine = r.mine.at[kind, m, here]
        mine[...] = result.astype(BF16)
        target = upstream if kind else x

        @pl.when(last if kind else first)
        def _():
            put(mine, target.at[rows], r.next_send.at[m], r.next_recv.at[m, c], near)

    def finish_parts(m, kind, parts):
        for c in parts:
            finish_part(m, kind, c)
        if PARTS - 1 in parts:
            take(r.came.at[kind, m], r.pair_send.at[kind, m])

    def finish(m):
        for kind, chosen in ((0, last), (1, first)):
            @pl.when(chosen)
            def _(kind=kind):
                finish_parts(m, kind, range(PARTS))

    def pass_on(m, target, parts):
        for c in parts:
            rows = target.at[part_of(m * SEQ + (1 - tensor) * OWN, c)]
            take(rows, r.next_recv.at[m, c])
            put(rows, rows, r.far_send.at[m], r.far_recv.at[m], partner)

    def arrived(m, target):
        take(target.at[pl.ds(0, OWN)], r.far_recv.at[m])

    def arrive(m, target):
        pass_on(m, target, range(PARTS))
        arrived(m, target)

    def tick(i, _):
        m = i

        def when(condition, action, *args):
            if isinstance(args[-1], range) and not args[-1]:
                return

            @pl.when(condition)
            def _():
                action(*args)

        def meanwhile(first_parts, next_parts, last_parts):
            when(jnp.logical_and(first, i == 1), finish_parts, 0, 0, first_parts)
            when(jnp.logical_and(last, i == 0), pass_on, 1, x, next_parts)
            when(jnp.logical_and(last, i == 1), finish_parts, 0, 1, last_parts)

        none = range(0)
        when(jnp.logical_and(last, i == 0), arrive, 0, x)
        when(jnp.logical_and(last, i == 1), arrived, 1, x)
        layer.norm(m)
        when(i == 0, take, r.qkv_w, load.at[1])
        layer.project(m)
        meanwhile(none, range(0, 2), none)
        layer.attend(m)
        meanwhile(range(0, 1), range(2, 5), range(0, 1))
        when(i == 0, take, out.at[pl.ds(4, 2)], load.at[2])
        layer.up(m)
        meanwhile(range(1, 4), range(5, PARTS), range(1, 3))

        @pl.when(jnp.logical_and(first, i == 0))
        def _():
            take(r.out_w, load.at[3])
            take(out.at[pl.ds(2, 2)], load.at[4])
            met(len(others))

        @pl.when(first)
        def _():
            layer.branches(m)
            meanwhile(range(4, PARTS), none, none)
            exchange(m, 0)

        @pl.when(last)
        def _():
            layer.back_gelu(m)
            layer.back_attend(m)
            meanwhile(none, none, range(3, 7))
            layer.back_inputs(m)
            meanwhile(none, none, range(7, PARTS))
            exchange(m, 1)

        return 0

    lax.fori_loop(0, 2, tick, 0)

    @pl.when(first)
    def _():
        finish_parts(1, 0, range(PARTS))
        arrive(0, upstream)
        layer.back_branches(0)
        layer.back_gelu(0)
        arrive(1, upstream)

    @pl.when(last)
    def _():
        finish_parts(1, 1, range(PARTS))

        def each(m, _):
            layer.branches(m)
            exchange(m, 0)
            return 0

        lax.fori_loop(0, 2, each, 0)

    grads = r.grads
    reduce = Reduce(place, grads, out, r.arrived, r.landing, r.send, r.recv)
    small = SmallReduce(place, r.small_mine, r.small_out, r.small_landing, r.small_pair,
                        r.small_send, r.small_recv)
    vectors, norms = r.vectors, r.norms

    def back(name):
        @pl.when(first)
        def _():
            if name == "back":
                layer.back_branches(1)
                layer.back_gelu(1)
                return

            def each(m, _):
                if name == "attend":
                    layer.back_attend(m)
                else:
                    layer.back_inputs(m)
                    exchange(m, 1)
                return 0

            lax.fori_loop(0, 2, each, 0)

    def sums():
        layer.bias_sums()
        norms[0] = vectors[pl.ds(0, 16)].astype(BF16)
        put(norms.at[0], norms.at[1], r.norms_sem.at[0], r.norms_sem.at[1], partner)
        r.small_mine[...] = vectors[...].astype(BF16)

    def norm_sums():
        take(norms.at[1], r.norms_sem.at[1])
        both = wide(norms.at[0]) + wide(norms.at[1])
        ln_row = lax.broadcasted_iota(jnp.int32, (16, COLS), 0) < 8
        r.small_mine[pl.ds(0, 16)] = jnp.where(ln_row, both, vectors[pl.ds(0, 16)]).astype(BF16)

    def copies():
        for m in range(2):
            for kind, final in ((0, r.y_out), (1, r.g_out)):
                rows = final.at[ds(m * SEQ + tensor * OWN, OWN)]
                mine = r.mine.at[kind, m]
                put(mine, rows, r.copy_send.at[kind, m], r.copy_recv.at[kind, m], partner)
                pltpu.make_async_copy(mine, rows, r.copy_own.at[kind, m]).start()

    for item in PLAN:
        if not isinstance(item, str):
            reduce.step(*item)
        elif item in ("back", "attend", "inputs"):
            back(item)
        elif item.startswith("finish"):
            finish(int(item[-1]))
        elif item.startswith("small"):
            small.step(int(item[-1]))
        elif item == "sums":
            sums()
        elif item == "norms":
            norm_sums()
        elif item == "copies":
            copies()
        else:
            layer.weight_sum(item)
    for s in range(SLABS):
        reduce.step(s, 10)
    for s in range(SLABS):
        reduce.drain(s)
    small.drain()
    take(norms.at[0], r.norms_sem.at[0])
    for m in range(2):
        for kind in range(2):
            take(r.mine.at[kind, m], r.copy_send.at[kind, m])
            take(r.mine.at[kind, m], r.copy_recv.at[kind, m])
            take(r.mine.at[kind, m], r.copy_own.at[kind, m])
        take(x.at[pl.ds(0, OWN)], r.next_send.at[m])
        take(x.at[pl.ds(0, OWN)], r.far_send.at[m])


def layer_call(*args):
    hbm, vmem = pl.BlockSpec(memory_space=pl.ANY), pl.BlockSpec(memory_space=pltpu.VMEM)
    smem = pl.BlockSpec(memory_space=pltpu.SMEM)
    rows = jax.ShapeDtypeStruct((TOKENS, WIDTH), BF16)
    return pl.pallas_call(
        layer_kernel,
        out_shape=(rows, rows, pltpu.VMEM((SLABS, SLAB_ROWS, COLS), BF16), pltpu.VMEM((SMALL, COLS), BF16)),
        in_specs=[hbm if name in IN_HBM else smem if name == "order" else vmem for name in INPUTS],
        out_specs=(hbm, hbm, vmem, vmem),
        scratch_shapes=list(SCRATCH.values()),
        compiler_params=pltpu.CompilerParams(
            collective_id=0, has_side_effects=True, vmem_limit_bytes=VMEM_LIMIT
        ),
    )(*args)


VECTORS = ((0, 2), (2, 2), (4, 2), (6, 2), (11, 2), (13, 4), (11, 2))


def widen_kernel(given, small, y_in, g_in, down, up, out, qkv, y_out, g_out, *rest):
    targets, (staged, held, rows, sems, copy_sems, row_sems) = rest[:8], rest[8:]
    passing = [(pltpu.make_async_copy(src, held.at[i], copy_sems.at[0, i]),
                pltpu.make_async_copy(held.at[i], dst, copy_sems.at[1, i]))
               for i, (src, dst) in enumerate(((y_in, y_out), (g_in, g_out)))]
    for come, _ in passing:
        come.start()
    values = small[...].astype(F32)
    moves = []
    for v, (row, count) in enumerate(VECTORS):
        for i in range(count):
            rows[v, :, pl.ds(i * COLS, COLS)] = values[row + i:row + i + 1]
        moves.append(pltpu.make_async_copy(rows.at[v, :, pl.ds(0, count * COLS)], targets[v], row_sems.at[v]))
    for t in range(3):
        moves.append(pltpu.make_async_copy(rows.at[7, :, pl.ds(t * COLS, COLS)], targets[7].at[t], row_sems.at[7 + t]))
        rows[7, :, pl.ds(t * COLS, COLS)] = values[8 + t:9 + t]
    for move in moves:
        move.start()

    def target(b):
        if b < 8:
            return down.at[pl.ds((b // 2) * COLS, COLS), pl.ds((b % 2) * COLS, COLS)]
        if b < 16:
            return up.at[pl.ds((b // 4 - 2) * COLS, COLS), pl.ds((b % 4) * COLS, COLS)]
        if b < 18:
            return out.at[:, pl.ds((b - 16) * COLS, COLS)]
        return qkv.at[(b - 18) % 3, pl.ds((b - 18) // 3 * COLS, COLS)]

    count, depth = SLABS * 4, 4
    copies = []
    for b in range(count):
        if b >= depth:
            copies[b - depth].wait()
        if b == 2 * depth:
            for come, go in passing:
                come.wait()
                go.start()
        slot = b % depth
        staged[slot] = given[b // 4, pl.ds((b % 4) * COLS, COLS)].astype(F32)
        copies.append(pltpu.make_async_copy(staged.at[slot], target(b), sems.at[slot]))
        copies[b].start()
    for b in range(count - depth, count):
        copies[b].wait()
    for move in moves + [go for _, go in passing]:
        move.wait()


def widened(grads, small, y, g):
    hbm, vmem = pl.BlockSpec(memory_space=pl.ANY), pl.BlockSpec(memory_space=pltpu.VMEM)
    shapes = [((2048, WIDTH), F32), ((WIDTH, 2048), F32), ((COLS, WIDTH), F32), ((3, WIDTH, COLS), F32),
              (y.shape, BF16), (g.shape, BF16)]
    shapes += [((1, rows * COLS), F32) for _, rows in VECTORS] + [((3, 1, COLS), F32)]
    grads, small = (pltpu.with_memory_space_constraint(a, pltpu.VMEM) for a in (grads, small))
    y, g = (pltpu.with_memory_space_constraint(a, pltpu.HBM) for a in (y, g))
    return pl.pallas_call(
        widen_kernel,
        out_shape=tuple(jax.ShapeDtypeStruct(shape, dtype) for shape, dtype in shapes),
        in_specs=[vmem, vmem] + [pl.BlockSpec(memory_space=pltpu.HBM)] * 2,
        out_specs=(hbm,) * 14,
        scratch_shapes=[pltpu.VMEM((4, COLS, COLS), F32), pltpu.VMEM((2, TOKENS, WIDTH), BF16),
                        pltpu.VMEM((8, 1, 4 * COLS), F32), DMA((4,)), DMA((2, 2)), DMA((10,))],
        compiler_params=pltpu.CompilerParams(vmem_limit_bytes=10 * 2**20),
    )(grads, small, y, g)


def shards(layer_input, cotangent, order, ln1_scale, ln1_bias, ln2_scale, ln2_bias, qkv_weight, qkv_bias,
           out_weight, out_bias, up_weight, up_bias, down_weight, down_bias):
    cos, low_sin, high_sin = (jnp.asarray(table) for table in rotary_tables())
    y, g, grads, small = layer_call(
        layer_input.reshape(TOKENS, WIDTH), cotangent.reshape(TOKENS, WIDTH), order,
        ln1_scale, ln1_bias, ln2_scale, ln2_bias,
        qkv_weight[0].transpose(1, 0, 2), qkv_bias[0], out_weight[0], out_bias, up_weight[0], up_bias,
        down_weight[0], down_bias, cos, low_sin, high_sin,
    )
    down, up, out, qkv, y, g, s1, b1, s2, b2, b_out, b_up, b_down, b_qkv = widened(grads, small, y, g)
    rows = (1, 2, 1, SEQ, WIDTH)
    return (y.reshape(rows), g.reshape(rows), s1, b1, s2, b2, qkv.transpose(1, 0, 2)[None], b_qkv.transpose(1, 0, 2),
            out[None], b_out, up[None], b_up, down[None], b_down)


def solution(mesh):
    return jax.shard_map(
        shards,
        mesh=mesh,
        in_specs=(
            P(None, "dp", None, None),
            P(None, "dp", None, None),
            P(),
            P("section", None),
            P("section", None),
            P("section", None),
            P("section", None),
            P("section", None, None, "tensor"),
            P("section", None, "tensor"),
            P("section", "tensor", None),
            P("section", None),
            P("section", None, "tensor"),
            P("section", "tensor"),
            P("section", "tensor", None),
            P("section", None),
        ),
        out_specs=(
            P("section", None, "dp", None, None),
            P("section", None, "dp", None, None),
            P("section", None),
            P("section", None),
            P("section", None),
            P("section", None),
            P("section", None, None, "tensor"),
            P("section", None, "tensor"),
            P("section", "tensor", None),
            P("section", None),
            P("section", None, "tensor"),
            P("section", "tensor"),
            P("section", "tensor", None),
            P("section", None),
        ),
        check_vma=False,
    )
```

profile of v0, /device:TPU:1, one launch (start us, length us, event | category | flops | bytes accessed | tf_op | source)
XLA Modules:
  0.0 157.8 jit_solution(18294816175389033413)
XLA Ops:
  0.7 147.6 %shard_map.281 = (bf16[512,1024]{1,0:T(8,128)(2,1)}, bf16[512,1024]{1,0:T(8,128)(2,1)}, bf16[6,2048,512]{2,1,0:T(8,128)(2,1)S(1)}, bf16[32,512]{1,0:T(8,128)(2,1)S(1)}) custom-call(bf16[512,1024]{1,0:T(8,128)(2,1)} %bitcast.25, bf16[512,1024]{1,0:T(8,128)(2,1)} %bitcast.26, s32[2]{0:T(128)} %refs_2_.1, bf16[1,1024]{1,0:T(2,128)(2,1)} %refs_3_.1, ...), custom_call_target="tpu_custom_call" | custom-call | tf_op jit(solution)/shard_map/pallas_call | solution.py:815
  148.3 9.3 %shard_map.282 = (f32[2048,1024]{1,0:T(8,128)}, f32[1024,2048]{1,0:T(8,128)}, f32[512,1024]{1,0:T(8,128)}, f32[3,1024,512]{2,1,0:T(8,128)}, bf16[512,1024]{1,0:T...) custom-call(bf16[6,2048,512]{2,1,0:T(8,128)(2,1)S(1)} %get-tuple-ele, ...), custom_call_target="tpu_custom_call" | custom-call | tf_op jit(solution)/shard_map/pallas_call | solution.py:884
where the time goes:
time: 158 us
  Pallas kernels  157 us (99%)
    pallas_call x1, Pallas kernels, layer_call(): pl.pallas_call(layer_kernel, out_shape=(rows, rows, pltpu.VMEM((SLABS, SL...  148 us
    pallas_call x1, Pallas kernels, widened(): pl.pallas_call(widen_kernel, out_shape=tuple((jax.ShapeDtypeStruct(shape,...  9.31 us

commit v1 on v0

--- a/solution.py
+++ b/solution.py
@@ -65,6 +65,8 @@
 
 
 def added(*parts):
+    if len(parts) == 2:
+        return parts[0] + parts[1]
     total = parts[0].astype(jnp.float32)
     for part in parts[1:]:
         total = total + part.astype(jnp.float32)
@@ -247,16 +249,17 @@
 
 
 PLAN = (
-    "down0", (0, 0), "down1", (1, 0), "back", (0, 1), "up0", (1, 1),
-    (2, 0), "up1", (3, 0), (0, 2), "attend", (2, 1), (1, 2), (3, 1),
-    (0, 3), "inputs", (2, 2), "last0", (1, 3), (4, 0), "last1", (3, 2),
-    (0, 4), (5, 0), "finish0", "finish1", "sums", "copies", (4, 1), (2, 3),
-    (1, 4), "norms", "small0", (5, 1), (3, 3), (0, 5), (4, 2), (2, 4),
-    (1, 5), (5, 2), (3, 4), (0, 6), "small1", (4, 3), (2, 5), (1, 6),
-    (5, 3), (3, 5), (0, 7), (4, 4), (2, 6), "small2", (1, 7), (5, 4),
-    (3, 6), (0, 8), (4, 5), (2, 7), (1, 8), (5, 5), "small3", (3, 7),
-    (0, 9), (4, 6), (2, 8), (1, 9), (5, 6), (3, 8), (4, 7), "small4",
-    (2, 9), (5, 7), (3, 9), (4, 8), (5, 8), (4, 9), (5, 9),
+    "down00", (0, 0), "down01", "down10", (1, 0), "down11", (0, 1), "back",
+    (1, 1), "up0", (2, 0), (0, 2), "up1", (3, 0), (2, 1), (1, 2),
+    "attend10", "attend11", "inputs10", (3, 1), "inputs11", "last0", (4, 0), (0, 3),
+    "last1", (5, 0), (2, 2), (4, 1), (1, 3), "sums", (5, 1), (3, 2),
+    (0, 4), (2, 3), (4, 2), (1, 4), "norms", "small0", (5, 2), (3, 3),
+    (0, 5), (2, 4), (4, 3), (1, 5), "finish0", (5, 3), (3, 4), "small1",
+    "finish1", (0, 6), "copies", (2, 5), (4, 4), (1, 6), (5, 4), (3, 5),
+    "small2", (0, 7), (2, 6), (4, 5), (1, 7), (5, 5), (3, 6), (0, 8),
+    (2, 7), "small3", (4, 6), (1, 8), (5, 6), (3, 7), (0, 9), (2, 8),
+    (4, 7), (1, 9), "small4", (5, 7), (3, 8), (2, 9), (4, 8), (5, 8),
+    (3, 9), (4, 9), (5, 9),
 )
 
 SEQ = 256
@@ -384,13 +387,13 @@
             self.activated[rows, lanes] = (hidden * cdf).astype(BF16)
             self.slope_block(m, n)[...] = (cdf + hidden * density).astype(BF16)
 
-    def branches(self, m):
-        rows = block(m, SEQ)
+    def branches(self, m, start=0, count=SEQ):
+        rows, here = ds(m * SEQ + start, count), ds(start, count)
         for j in range(2):
             lanes = pl.ds(j * COLS, COLS)
             total = nn(self.context[rows], self.out_w[:, lanes])
             total = total + nn(self.activated[rows], self.out[2 + j])
-            self.partial[m, :, lanes] = total.astype(BF16)
+            self.partial[m, here, lanes] = total.astype(BF16)
 
     def back_branches(self, m):
         rows = block(m, SEQ)
@@ -409,10 +412,10 @@
                 wide(self.d_hidden.at[rows, lanes]) * wide(self.slope_block(m, n))
             ).astype(BF16)
 
-    def back_attend(self, m):
+    def back_attend(self, m, pairs=range(4)):
         rows = block(m, SEQ)
         tables = (self.cos[...], self.low_sin[...], self.high_sin[...])
-        for hp in range(4):
+        for hp in pairs:
             lanes = pl.ds(hp * 128, 128)
             q, k, v = (self.qkv[t, rows, lanes] for t in range(3))
             d_context = self.d_context[rows, lanes]
@@ -433,10 +436,10 @@
             for t, part in enumerate((d_query, d_key, d_value)):
                 self.d_projected[t, rows, lanes] = part.astype(BF16)
 
-    def back_inputs(self, m):
-        rows = block(m, SEQ)
+    def back_inputs(self, m, halves=range(2), start=0, count=SEQ):
+        rows, here = ds(m * SEQ + start, count), ds(start, count)
         mean, rstd = self.mean[rows], self.rstd[rows]
-        for j in range(2):
+        for j in halves:
             lanes = pl.ds(j * COLS, COLS)
             d_second = None
             for n in range(4):
@@ -452,7 +455,7 @@
                 row = pl.ds(2 * i + j, 1)
                 self.vectors[row] = self.vectors[row] + jnp.sum(value, axis=0, keepdims=True)
             d_normed = d_first * wide(self.ln1_scale.at[:, lanes]) + d_second * wide(self.ln2_scale.at[:, lanes])
-            self.partial[m, :, lanes] = d_normed.astype(BF16)
+            self.partial[m, here, lanes] = d_normed.astype(BF16)
 
     def weight_sum(self, name):
         def product(left, columns, targets):
@@ -461,9 +464,11 @@
                 self.grads[b // 4, pl.ds((b % 4) * COLS, COLS)] = nn(turned, right).astype(BF16)
 
         upstream = [self.upstream[:, pl.ds(c * COLS, COLS)] for c in range(2)]
-        if name in ("down0", "down1"):
-            for r in (0, 1) if name == "down0" else (2, 3):
-                product(self.activated, pl.ds(r * COLS, COLS), [(upstream[c], 2 * r + c) for c in range(2)])
+        if name.startswith("down"):
+            slab, half = int(name[-2]), self.core if int(name[-1]) else 1 - self.core
+            turned = self.activated[:, ds((2 * slab + half) * COLS, COLS)].T
+            for c in range(2):
+                self.grads[slab, ds((2 * half + c) * COLS, COLS)] = nn(turned, upstream[c]).astype(BF16)
         elif name in ("up0", "up1"):
             r = int(name == "up1")
             d_hidden = [self.d_hidden[:, pl.ds(n * COLS, COLS)] for n in range(4)]
@@ -544,8 +549,8 @@
 def layer_kernel(*refs):
     names = INPUTS + OUTPUTS + tuple(SCRATCH)
     r = Refs(zip(names, refs))
-    layer = Layer(vars(r))
-    place = Place()
+    layer, place = Layer(vars(r)), Place()
+    layer.core = place.core
     section, tensor = place.section, place.tensor
     first, last = section == 0, section == 1
     dp = lax.axis_index("dp")
@@ -603,6 +608,8 @@
         met(len(others))
 
     r.vectors[...] = jnp.zeros((SMALL, COLS), F32)
+
+    own_half, other_half = tensor * OWN, (1 - tensor) * OWN
 
     def part_of(start, c):
         return ds(start + c * PART, PART)
@@ -686,7 +693,7 @@
         meanwhile(range(0, 1), range(2, 5), range(0, 1))
         when(i == 0, take, out.at[pl.ds(4, 2)], load.at[2])
         layer.up(m)
-        meanwhile(range(1, 4), range(5, PARTS), range(1, 3))
+        meanwhile(range(1, 4), range(5, PARTS), range(1, 4))
 
         @pl.when(jnp.logical_and(first, i == 0))
         def _():
@@ -696,17 +703,17 @@
 
         @pl.when(first)
         def _():
-            layer.branches(m)
+            layer.branches(m, other_half, OWN)
             meanwhile(range(4, PARTS), none, none)
             exchange(m, 0)
+            layer.branches(m, own_half, OWN)
 
         @pl.when(last)
         def _():
             layer.back_gelu(m)
             layer.back_attend(m)
-            meanwhile(none, none, range(3, 7))
+            meanwhile(none, none, range(4, PARTS))
             layer.back_inputs(m)
-            meanwhile(none, none, range(7, PARTS))
             exchange(m, 1)
 
         return 0
@@ -719,7 +726,16 @@
         arrive(0, upstream)
         layer.back_branches(0)
         layer.back_gelu(0)
-        arrive(1, upstream)
+        layer.back_attend(0, range(0, 2))
+        pass_on(1, upstream, range(0, 1))
+        layer.back_attend(0, range(2, 4))
+        pass_on(1, upstream, range(1, 3))
+        layer.back_inputs(0, range(0, 1))
+        pass_on(1, upstream, range(3, 5))
+        layer.back_inputs(0, range(1, 2))
+        pass_on(1, upstream, range(5, PARTS))
+        exchange(0, 1)
+        arrived(1, upstream)
 
     @pl.when(last)
     def _():
@@ -745,16 +761,13 @@
                 layer.back_branches(1)
                 layer.back_gelu(1)
                 return
-
-            def each(m, _):
-                if name == "attend":
-                    layer.back_attend(m)
-                else:
-                    layer.back_inputs(m)
+            m, half = int(name[-2]), int(name[-1])
+            if name.startswith("attend"):
+                layer.back_attend(m, range(2 * half, 2 * half + 2))
+            else:
+                layer.back_inputs(m, range(half, half + 1))
+                if half:
                     exchange(m, 1)
-                return 0
-
-            lax.fori_loop(0, 2, each, 0)
 
     def sums():
         layer.bias_sums()
@@ -779,7 +792,7 @@
     for item in PLAN:
         if not isinstance(item, str):
             reduce.step(*item)
-        elif item in ("back", "attend", "inputs"):
+        elif item[:4] in ("back", "atte", "inpu"):
             back(item)
         elif item.startswith("finish"):
             finish(int(item[-1]))

time: 158 us -> 155 us (0.981)
  Pallas kernels: 157 us -> 154 us
    pallas_call x1, Pallas kernels: 148 us -> 144 us  [layer_call(): pl.pallas_call(layer_kernel, out_shape=(rows, rows, pltpu.VMEM((SLABS, SL...]
where the time goes in v1:
time: 155 us
  Pallas kernels  154 us (99%)
    pallas_call x1, Pallas kernels, layer_call(): pl.pallas_call(layer_kernel, out_shape=(rows, rows, pltpu.VMEM((SLABS, SL...  144 us
    pallas_call x1, Pallas kernels, widened(): pl.pallas_call(widen_kernel, out_shape=tuple((jax.ShapeDtypeStruct(shape,...  9.31 us

profile of v1, /device:TPU:1, one launch (start us, length us, event | category | flops | bytes accessed | tf_op | source)
XLA Modules:
  0.0 154.5 jit_solution(17998235494690295685)
XLA Ops:
  0.7 144.4 %shard_map.281 = (bf16[512,1024]{1,0:T(8,128)(2,1)}, bf16[512,1024]{1,0:T(8,128)(2,1)}, bf16[6,2048,512]{2,1,0:T(8,128)(2,1)S(1)}, bf16[32,512]{1,0:T(8,128)(2,1)S(1)}) custom-call(bf16[512,1024]{1,0:T(8,128)(2,1)} %bitcast.25, bf16[512,1024]{1,0:T(8,128)(2,1)} %bitcast.26, s32[2]{0:T(128)} %refs_2_.1, bf16[1,1024]{1,0:T(2,128)(2,1)} %refs_3_.1, ...), custom_call_target="tpu_custom_call" | custom-call | tf_op jit(solution)/shard_map/pallas_call | solution.py:828
  145.0 9.3 %shard_map.282 = (f32[2048,1024]{1,0:T(8,128)}, f32[1024,2048]{1,0:T(8,128)}, f32[512,1024]{1,0:T(8,128)}, f32[3,1024,512]{2,1,0:T(8,128)}, bf16[512,1024]{1,0:T...) custom-call(bf16[6,2048,512]{2,1,0:T(8,128)(2,1)S(1)} %get-tuple-ele, ...), custom_call_target="tpu_custom_call" | custom-call | tf_op jit(solution)/shard_map/pallas_call | solution.py:897

commit v2 on v1

--- a/solution.py
+++ b/solution.py
@@ -250,16 +250,16 @@
 
 PLAN = (
     "down00", (0, 0), "down01", "down10", (1, 0), "down11", (0, 1), "back",
-    (1, 1), "up0", (2, 0), (0, 2), "up1", (3, 0), (2, 1), (1, 2),
-    "attend10", "attend11", "inputs10", (3, 1), "inputs11", "last0", (4, 0), (0, 3),
-    "last1", (5, 0), (2, 2), (4, 1), (1, 3), "sums", (5, 1), (3, 2),
-    (0, 4), (2, 3), (4, 2), (1, 4), "norms", "small0", (5, 2), (3, 3),
-    (0, 5), (2, 4), (4, 3), (1, 5), "finish0", (5, 3), (3, 4), "small1",
-    "finish1", (0, 6), "copies", (2, 5), (4, 4), (1, 6), (5, 4), (3, 5),
-    "small2", (0, 7), (2, 6), (4, 5), (1, 7), (5, 5), (3, 6), (0, 8),
-    (2, 7), "small3", (4, 6), (1, 8), (5, 6), (3, 7), (0, 9), (2, 8),
-    (4, 7), (1, 9), "small4", (5, 7), (3, 8), (2, 9), (4, 8), (5, 8),
-    (3, 9), (4, 9), (5, 9),
+    (1, 1), "up0", (2, 0), (0, 2), "up1", (3, 0), (2, 1), "attend00",
+    (1, 2), "attend01", (3, 1), "inputs00", "inputs01", (0, 3), "attend10", "attend11",
+    (1, 3), "inputs10", (2, 2), "inputs11", (3, 2), (0, 4), (1, 4), "last0",
+    (4, 0), "last1", (5, 0), (2, 3), (4, 1), (3, 3), "sums", (5, 1),
+    (0, 5), (1, 5), (2, 4), (4, 2), (3, 4), "norms", "small0", (5, 2),
+    (0, 6), (1, 6), (2, 5), (4, 3), (3, 5), "finish0", (5, 3), (0, 7),
+    "small1", "finish1", (1, 7), "copies", (2, 6), (4, 4), (3, 6), (5, 4),
+    (0, 8), "small2", (1, 8), (2, 7), (4, 5), (3, 7), (5, 5), (0, 9),
+    (1, 9), (2, 8), "small3", (4, 6), (3, 8), (5, 6), (2, 9), (4, 7),
+    (3, 9), (5, 7), (4, 8), "small4", (5, 8), (4, 9), (5, 9),
 )
 
 SEQ = 256
@@ -726,15 +726,7 @@
         arrive(0, upstream)
         layer.back_branches(0)
         layer.back_gelu(0)
-        layer.back_attend(0, range(0, 2))
-        pass_on(1, upstream, range(0, 1))
-        layer.back_attend(0, range(2, 4))
-        pass_on(1, upstream, range(1, 3))
-        layer.back_inputs(0, range(0, 1))
-        pass_on(1, upstream, range(3, 5))
-        layer.back_inputs(0, range(1, 2))
-        pass_on(1, upstream, range(5, PARTS))
-        exchange(0, 1)
+        pass_on(1, upstream, range(PARTS))
         arrived(1, upstream)
 
     @pl.when(last)

time: 155 us -> 152 us (0.981)
  Pallas kernels: 154 us -> 151 us
    pallas_call x1, Pallas kernels: 144 us -> 142 us  [layer_call(): pl.pallas_call(layer_kernel, out_shape=(rows, rows, pltpu.VMEM((SLABS, SL...]
where the time goes in v2:
time: 152 us
  Pallas kernels  151 us (99%)
    pallas_call x1, Pallas kernels, layer_call(): pl.pallas_call(layer_kernel, out_shape=(rows, rows, pltpu.VMEM((SLABS, SL...  142 us
    pallas_call x1, Pallas kernels, widened(): pl.pallas_call(widen_kernel, out_shape=tuple((jax.ShapeDtypeStruct(shape,...  9.31 us

profile of v2, /device:TPU:1, one launch (start us, length us, event | category | flops | bytes accessed | tf_op | source)
XLA Modules:
  0.0 152.2 jit_solution(17854071857333425791)
XLA Ops:
  0.7 142.1 %shard_map.281 = (bf16[512,1024]{1,0:T(8,128)(2,1)}, bf16[512,1024]{1,0:T(8,128)(2,1)}, bf16[6,2048,512]{2,1,0:T(8,128)(2,1)S(1)}, bf16[32,512]{1,0:T(8,128)(2,1)S(1)}) custom-call(bf16[512,1024]{1,0:T(8,128)(2,1)} %bitcast.25, bf16[512,1024]{1,0:T(8,128)(2,1)} %bitcast.26, s32[2]{0:T(128)} %refs_2_.1, bf16[1,1024]{1,0:T(2,128)(2,1)} %refs_3_.1, ...), custom_call_target="tpu_custom_call" | custom-call | tf_op jit(solution)/shard_map/pallas_call | solution.py:820
  142.8 9.3 %shard_map.282 = (f32[2048,1024]{1,0:T(8,128)}, f32[1024,2048]{1,0:T(8,128)}, f32[512,1024]{1,0:T(8,128)}, f32[3,1024,512]{2,1,0:T(8,128)}, bf16[512,1024]{1,0:T...) custom-call(bf16[6,2048,512]{2,1,0:T(8,128)(2,1)S(1)} %get-tuple-ele, ...), custom_call_target="tpu_custom_call" | custom-call | tf_op jit(solution)/shard_map/pallas_call | solution.py:889

commit v3 on v2

--- a/solution.py
+++ b/solution.py
@@ -250,16 +250,16 @@
 
 PLAN = (
     "down00", (0, 0), "down01", "down10", (1, 0), "down11", (0, 1), "back",
-    (1, 1), "up0", (2, 0), (0, 2), "up1", (3, 0), (2, 1), "attend00",
-    (1, 2), "attend01", (3, 1), "inputs00", "inputs01", (0, 3), "attend10", "attend11",
-    (1, 3), "inputs10", (2, 2), "inputs11", (3, 2), (0, 4), (1, 4), "last0",
-    (4, 0), "last1", (5, 0), (2, 3), (4, 1), (3, 3), "sums", (5, 1),
-    (0, 5), (1, 5), (2, 4), (4, 2), (3, 4), "norms", "small0", (5, 2),
-    (0, 6), (1, 6), (2, 5), (4, 3), (3, 5), "finish0", (5, 3), (0, 7),
-    "small1", "finish1", (1, 7), "copies", (2, 6), (4, 4), (3, 6), (5, 4),
-    (0, 8), "small2", (1, 8), (2, 7), (4, 5), (3, 7), (5, 5), (0, 9),
-    (1, 9), (2, 8), "small3", (4, 6), (3, 8), (5, 6), (2, 9), (4, 7),
-    (3, 9), (5, 7), (4, 8), "small4", (5, 8), (4, 9), (5, 9),
+    (1, 1), "up0", (2, 0), (0, 2), "up1", (3, 0), (2, 1), "attend01",
+    (1, 2), (3, 1), "inputs00", "inputs01", "attend10", (0, 3), "attend11", "inputs10",
+    (1, 3), "inputs11", (2, 2), "last0", (4, 0), (3, 2), (0, 4), (1, 4),
+    "last1", (5, 0), (4, 1), (2, 3), (5, 1), "sums", (3, 3), (0, 5),
+    (1, 5), (4, 2), (2, 4), (5, 2), "norms", "small0", (3, 4), (0, 6),
+    (1, 6), (4, 3), (2, 5), (5, 3), "finish0", (3, 5), (0, 7), "small1",
+    "finish1", (1, 7), "copies", (4, 4), (2, 6), (5, 4), (3, 6), (0, 8),
+    "small2", (1, 8), (4, 5), (2, 7), (5, 5), (3, 7), (0, 9), (1, 9),
+    (4, 6), "small3", (2, 8), (5, 6), (3, 8), (4, 7), (2, 9), (5, 7),
+    (3, 9), (4, 8), "small4", (5, 8), (4, 9), (5, 9),
 )
 
 SEQ = 256
@@ -712,8 +712,8 @@
         def _():
             layer.back_gelu(m)
             layer.back_attend(m)
+            layer.back_inputs(m)
             meanwhile(none, none, range(4, PARTS))
-            layer.back_inputs(m)
             exchange(m, 1)
 
         return 0
@@ -723,10 +723,12 @@
     @pl.when(first)
     def _():
         finish_parts(1, 0, range(PARTS))
-        arrive(0, upstream)
+        pass_on(0, upstream, range(PARTS))
+        pass_on(1, upstream, range(PARTS))
+        arrived(0, upstream)
         layer.back_branches(0)
         layer.back_gelu(0)
-        pass_on(1, upstream, range(PARTS))
+        layer.back_attend(0, range(0, 2))
         arrived(1, upstream)
 
     @pl.when(last)

time: 152 us -> 154 us (1.013)
  Pallas kernels: 151 us -> 153 us
where the time goes in v3:
time: 154 us
  Pallas kernels  153 us (99%)
    pallas_call x1, Pallas kernels, layer_call(): pl.pallas_call(layer_kernel, out_shape=(rows, rows, pltpu.VMEM((SLABS, SL...  143 us
    pallas_call x1, Pallas kernels, widened(): pl.pallas_call(widen_kernel, out_shape=tuple((jax.ShapeDtypeStruct(shape,...  9.31 us

profile of v3, /device:TPU:1, one launch (start us, length us, event | category | flops | bytes accessed | tf_op | source)
XLA Modules:
  0.0 153.6 jit_solution(15126658622894108825)
XLA Ops:
  0.7 143.5 %shard_map.281 = (bf16[512,1024]{1,0:T(8,128)(2,1)}, bf16[512,1024]{1,0:T(8,128)(2,1)}, bf16[6,2048,512]{2,1,0:T(8,128)(2,1)S(1)}, bf16[32,512]{1,0:T(8,128)(2,1)S(1)}) custom-call(bf16[512,1024]{1,0:T(8,128)(2,1)} %bitcast.25, bf16[512,1024]{1,0:T(8,128)(2,1)} %bitcast.26, s32[2]{0:T(128)} %refs_2_.1, bf16[1,1024]{1,0:T(2,128)(2,1)} %refs_3_.1, ...), custom_call_target="tpu_custom_call" | custom-call | tf_op jit(solution)/shard_map/pallas_call | solution.py:822
  144.1 9.3 %shard_map.282 = (f32[2048,1024]{1,0:T(8,128)}, f32[1024,2048]{1,0:T(8,128)}, f32[512,1024]{1,0:T(8,128)}, f32[3,1024,512]{2,1,0:T(8,128)}, bf16[512,1024]{1,0:T...) custom-call(bf16[6,2048,512]{2,1,0:T(8,128)(2,1)S(1)} %get-tuple-ele, ...), custom_call_target="tpu_custom_call" | custom-call | tf_op jit(solution)/shard_map/pallas_call | solution.py:891
